TPU v7x, 32 devices: a whole 2x2x4 slice. The times are simulated.
32 devices in a mesh: ka: 4 (over y, x), band: 8 (over z, core).
Axes of the slice: x: 2, y: 2, z: 4, core: 2. Of those that a mesh axis runs over, the one named last changes fastest.
Arguments:
- targets: bfloat16 [4, 8, 24, 24, 128], P('ka', 'band'), may hold values from -6 to 6
- occupied: bfloat16 [4, 16, 24, 24, 128], P('ka', 'band'), may hold values from -6 to 6
- wavevectors: int32 [4, 3], replicated, may hold values from 0 to 3
- umklapp: int32 [4, 2, 3], P('ka'), may hold values from -1 to 1
- owners: int32 [4, 2, 2], P('ka'), may hold values from 0 to 7
Outputs:
- exchange: bfloat16 [4, 8, 24, 24, 128], P('ka', 'band')
All inputs are finite; a program needn't handle non-finite values.
Results may differ from a plain program's by a relative error of at most 0.017.
Values may be sent and summed in bfloat16 or wider, within the bound.
A program may use at most 64 MiB of HBM per device.

v0:
```python
import math

import jax
import jax.numpy as jnp
from jax import lax
from jax.sharding import PartitionSpec as P

OCC_DEV = 2
STEPS = 2
KGRID = 4


screening_sq = 0.16
spacing = 0.25
prefactor = -0.5


def from_behind(block, axis, distance):
    devices = range(lax.axis_size(axis))
    route = [((i - distance) % len(devices), i) for i in devices]
    return lax.ppermute(block, axis, route)


def spread(block, axis, holder):
    block = jnp.where(lax.axis_index(axis) == holder, block, jnp.zeros_like(block))
    return lax.psum(block, axis)


def tables(length):
    indices = jnp.arange(length, dtype=jnp.int32)
    products = indices[:, None] * indices[None, :] % length
    angles = products.astype(jnp.float32) * (2.0 * math.pi / length)
    return (jnp.cos(angles), jnp.sin(angles))


def last_matrix(length, sign_value):
    cosine, sine_table = tables(length)
    upper_rows = jnp.concatenate([cosine, -sign_value * sine_table], axis=1)
    bottom = jnp.concatenate([sign_value * sine_table, cosine], axis=1)
    return jnp.concatenate([upper_rows, bottom], axis=0).astype(jnp.bfloat16)


def stacked_table(length):
    cosine, sine_table = tables(length)
    return jnp.concatenate([cosine, sine_table], axis=0).astype(jnp.bfloat16)


def along_axis(grid_values, spec, length, sign_value, axis_pos):
    both = jnp.einsum(spec, stacked_table(length), grid_values, preferred_element_type=jnp.float32)
    cos_part = lax.slice_in_dim(both, 0, length, axis=axis_pos)
    sin_part = lax.slice_in_dim(both, length, 2 * length, axis=axis_pos)
    half_width = both.shape[-1] // 2
    swapped = jnp.concatenate([sin_part[..., half_width:], sin_part[..., :half_width]], axis=-1)
    half_sign = jnp.concatenate(
        [jnp.ones((half_width,), jnp.float32), -jnp.ones((half_width,), jnp.float32)]
    )
    return (cos_part + sign_value * half_sign * swapped).astype(jnp.bfloat16)


def fourier(grid_values, sign_value):
    last_width = grid_values.shape[-1]
    flattened = grid_values.reshape(-1, last_width)
    moved = jnp.dot(
        flattened, last_matrix(last_width // 2, sign_value), preferred_element_type=jnp.float32
    )
    grid_values = moved.astype(jnp.bfloat16).reshape(grid_values.shape)
    grid_values = along_axis(grid_values, "vy,byzc->bvzc", grid_values.shape[1], sign_value, 1)
    grid_values = along_axis(grid_values, "vz,byzc->byvc", grid_values.shape[2], sign_value, 2)
    return grid_values


def coulomb(shift_vec, grid_x, grid_y, grid_z):
    squares = []
    for axis_pos, length in ((0, grid_x), (1, grid_y), (2, grid_z)):
        indices = jnp.arange(length, dtype=jnp.int32)
        signed = jnp.where(indices * 2 < length, indices, indices - length)
        wavenumber = (
            2.0 * math.pi / (length * spacing) * (signed.astype(jnp.float32) + shift_vec[axis_pos])
        )
        squares.append(wavenumber * wavenumber)
    square_x = jnp.concatenate([squares[0], squares[0]])
    total_sq = (
        squares[1][:, None, None]
        + squares[2][None, :, None]
        + square_x[None, None, :]
        + screening_sq
    )
    return 4.0 * math.pi / total_sq


def pair_density(visitor, resident):
    half_width = visitor.shape[-1] // 2
    visit_re = visitor[..., :half_width].astype(jnp.float32)
    visit_im = visitor[..., half_width:].astype(jnp.float32)
    res_re = resident[..., :half_width].astype(jnp.float32)
    res_im = resident[..., half_width:].astype(jnp.float32)
    real_part = visit_re * res_re + visit_im * res_im
    imag_part = visit_re * res_im - visit_im * res_re
    return jnp.concatenate([real_part, imag_part], axis=-1).astype(jnp.bfloat16)


def apply_potential(visitor, potential):
    half_width = visitor.shape[-1] // 2
    visit_re = visitor[..., :half_width].astype(jnp.float32)
    visit_im = visitor[..., half_width:].astype(jnp.float32)
    pot_re = potential[..., :half_width].astype(jnp.float32)
    pot_im = potential[..., half_width:].astype(jnp.float32)
    real_part = visit_re * pot_re - visit_im * pot_im
    imag_part = visit_re * pot_im + visit_im * pot_re
    return jnp.concatenate([real_part, imag_part], axis=-1)


def exchange_term(visitor, resident, kernel, cells):
    density = pair_density(visitor, resident)
    spectrum = fourier(density, 1.0)
    screened = (spectrum.astype(jnp.float32) * kernel * (1.0 / cells)).astype(jnp.bfloat16)
    potential = fourier(screened, -1.0)
    return apply_potential(visitor, potential)


def local(targets, occupied, wavevectors, umklapp, owners):
    resident = targets[0]
    grid_y, grid_z, last_width = (resident.shape[1], resident.shape[2], resident.shape[3])
    grid_x = last_width // 2
    cells = float(grid_x * grid_y * grid_z)
    ka_position = lax.axis_index("ka")
    k_total = lax.axis_size("ka")
    own_coords = lax.dynamic_index_in_dim(wavevectors, ka_position, 0, keepdims=False)
    accumulated = jnp.zeros(resident.shape, jnp.float32)
    visiting = occupied[0]
    for section_index in range(1, STEPS + 1):
        visit_index = (ka_position - section_index) % k_total
        visit_coords = lax.dynamic_index_in_dim(wavevectors, visit_index, 0, keepdims=False)
        shift_vec = (own_coords - visit_coords).astype(jnp.float32) / KGRID + umklapp[
            0, section_index - 1
        ].astype(jnp.float32)
        kernel = coulomb(shift_vec, grid_x, grid_y, grid_z)
        visiting = from_behind(visiting, "ka", 1)
        for slot_index in range(OCC_DEV):
            owner_band = owners[0, section_index - 1, slot_index]
            visitor = spread(visiting[slot_index], "band", owner_band)
            accumulated = accumulated + exchange_term(visitor, resident, kernel, cells)
    return (prefactor * accumulated).astype(jnp.bfloat16)[None]


def solution(mesh):
    placed = (
        P("ka", "band", None, None, None),
        P("ka", "band", None, None, None),
        P(),
        P("ka", None, None),
        P("ka", None, None),
    )
    return jax.shard_map(
        local,
        mesh=mesh,
        in_specs=placed,
        out_specs=P("ka", "band", None, None, None),
        check_vma=False,
    )
```

profile of v0, /device:TPU:0, one launch (start us, length us, event | category | flops | bytes accessed | tf_op | source)
XLA Modules:
  0.0 113.4 jit_solution(15903285461165056261)
XLA Ops:
  6.5 1.0 copy.122
  7.6 3.0 %collective-permute-start = (bf16[2,24,24,128]{3,1,2,0:T(8,128)(2,1)S(1)}, bf16[2,24,24,128]{3,1,2,0:T(8,128)(2,1)S(1)}, u32[]{:S(2)}, u32[]{:S(2)}) collective-permute-start(bf16[2,24,24,128]{3,1,2,0:T(8,128)(2,1)S(1)} %bitcast.304), channel_id=1, source_target_pairs={{24,0},{0,8},{8,16},{16,24},{25,1},{1,9},{9,17},{17,25},{26,2},{2,... | collective-permute-start | bytes 884744 | tf_op jit(solution)/shard_map/ppermute | solution.py:21
  11.0 0.7 fusion.151
  14.3 0.7 copy-done.8
  15.0 0.7 fusion.152
  15.6 0.6 multiply_multiply_fusion.1
  16.3 0.7 multiply_multiply_fusion.2
  16.9 0.6 multiply_multiply_fusion
  17.6 0.6 multiply_multiply_fusion.4
  18.4 0.6 multiply_multiply_fusion.5
  19.0 1.5 %collective-permute-start.1 = (bf16[2,24,24,128]{3,1,2,0:T(8,128)(2,1)S(1)}, bf16[2,24,24,128]{3,1,2,0:T(8,128)(2,1)S(1)}, u32[]{:S(2)}, u32[]{:S(2)}) collective-permute-start(bf16[2,24,24,128]{3,1,2,0:T(8,128)(2,1)S(1)} %collective-permute-done), channel_id=1, source_target_pairs={{24,0},{0,8},{8,16},{16,24},{25,1},{1,9},{9,17},{17,25},{26,2},{2,... | collective-permute-start | bytes 884744 | tf_op jit(solution)/shard_map/ppermute | solution.py:21
  20.5 0.6 multiply_multiply_fusion.3
  21.1 0.7 fusion.62
  21.9 6.5 %collective-permute-done.1 = bf16[2,24,24,128]{3,1,2,0:T(8,128)(2,1)S(1)} collective-permute-done((bf16[2,24,24,128]{3,1,2,0:T(8,128)(2,1)S(1)}, bf16[2,24,24,128]{3,1,2,0:T(8,128)(2,1)S(1)}, u32[]{:S(2)}, u32[]{:S(2)}) %collective-permute-start.1) | collective-permute-done | bytes 294944 | tf_op jit(solution)/shard_map/ppermute | solution.py:21
  28.4 0.7 fusion.60
  29.3 57.3 %all-reduce.3.cloned.1.call-done = (bf16[24,24,128]{2,0,1:T(8,128)(2,1)}, bf16[24,24,128]{2,0,1:T(8,128)(2,1)}, bf16[24,24,128]{2,0,1:T(8,128)(2,1)}, bf16[24,24,128]{2,0,1:T(8,128)(2,1)}) async-done(((bf16[24,24,128]{2,0,1:T(8,128)(2,1)}, bf16[24,24,128]{2,0,1:T(8,128)(2,1)}, bf16[24,24,128]{2,0,1:T(8,128)(2,1)}, bf16[24,24,128]{2,0,1:T(8,128)(2,1)}), (bf16[24,24,128]{2,0,1:T(8,128)(2,1)}, ...) | async-done | bytes 589840 | tf_op jit(solution)/shard_map/psum | solution.py:26
  86.6 1.4 %fusion.21 = (bf16[1,24,24,64]{3,1,2,0:T(8,128)(2,1)S(1)}, bf16[1,24,24,64]{3,1,2,0:T(8,128)(2,1)S(1)}, bf16[1,24,24,64]{3,1,2,0:T(8,128)(2,1)S(1)}, bf16[1,24,24,64]{3,1,2,0:T(8,128)(2,1)S(1)}) fusion(bf16[24,24,128]{2,0,1:T(8,128)(2,1)} %get-tuple-element.6, bf16[1,24,24,128]{3,1,2,0:T(8,128)(2,1)S(1)} %bitcast.282, bf16[24,24,128]{2,0,1:T(8,128)(2,1)} %get-tuple-element.5), kind=kLoop, calls=%fused_computation.77 | loop fusion | flops 811008 | bytes 737280 | tf_op jit(solution)/shard_map/convert.19
  89.5 0.7 copy-done.1
  92.2 0.6 copy-done.6
  94.3 0.5 multiply_convert_fusion
  97.8 0.6 copy-done.5
  103.5 0.7 copy-done.2
  104.6 0.7 copy-done
  105.9 0.7 copy.71
  (98 shorter events, 14.3 us)
Async XLA Ops:
  6.5 80.1 %all-reduce.3.cloned.1.call-start = ((), (), s32[]{:S(2)}) async-start(), calls=%async_computation | async-start | bytes 1179648 | tf_op jit(solution)/shard_map/psum | solution.py:26
  6.5 4.5 %copy-start.7 = (s32[1,2,2]{2,1,0:T(2,128)S(1)}, s32[1,2,2]{2,1,0:T(2,128)}, u32[]{:S(2)}) copy-start(s32[1,2,2]{2,1,0:T(2,128)} %param.9) | copy-start | bytes 52
  7.6 6.6 %copy-start.4 = (bf16[1,1,24,24,128]{4,3,2,1,0:T(8,128)(2,1)S(1)}, bf16[1,1,24,24,128]{4,3,2,1,0:T(8,128)(2,1)}, u32[]{:S(2)}) copy-start(bf16[1,1,24,24,128]{4,3,2,1,0:T(8,128)(2,1)} %param.5) | copy-start | bytes 442372
  7.6 11.4 %collective-permute-start = (bf16[2,24,24,128]{3,1,2,0:T(8,128)(2,1)S(1)}, bf16[2,24,24,128]{3,1,2,0:T(8,128)(2,1)S(1)}, u32[]{:S(2)}, u32[]{:S(2)}) collective-permute-start(bf16[2,24,24,128]{3,1,2,0:T(8,128)(2,1)S(1)} %bitcast.304), channel_id=1, source_target_pairs={{24,0},{0,8},{8,16},{16,24},{25,1},{1,9},{9,17},{17,25},{26,2},{2,... | collective-permute-start | bytes 884744 | tf_op jit(solution)/shard_map/ppermute | solution.py:21
  14.2 0.7 copy-start.8
  14.3 0.7 copy-start.9
  19.0 9.4 %collective-permute-start.1 = (bf16[2,24,24,128]{3,1,2,0:T(8,128)(2,1)S(1)}, bf16[2,24,24,128]{3,1,2,0:T(8,128)(2,1)S(1)}, u32[]{:S(2)}, u32[]{:S(2)}) collective-permute-start(bf16[2,24,24,128]{3,1,2,0:T(8,128)(2,1)S(1)} %collective-permute-done), channel_id=1, source_target_pairs={{24,0},{0,8},{8,16},{16,24},{25,1},{1,9},{9,17},{17,25},{26,2},{2,... | collective-permute-start | bytes 884744 | tf_op jit(solution)/shard_map/ppermute | solution.py:21
  89.4 0.9 copy-start.1
  89.4 1.0 copy-start.3
  92.2 0.7 copy-start.6
  97.8 0.7 copy-start.5
  103.3 0.9 copy-start.2
  104.4 0.9 copy-start
Sparse Core Ops, SparseCore 0:
  29.3 57.2 all-reduce.2
where the time goes:
time: 114 us; the launch traced here: 113 us
  waiting for transfers between devices  63.8 us (56%)
  between operations  16.6 us (15%)
  local copies, waits for them, and re-layouts  11.3 us (10%)
  other arithmetic  10.8 us (9%)
  matrix products  6.39 us (6%)
  starting transfers between devices  4.49 us (4%)
    psum x1, waiting for transfers between devices, spread(): return lax.psum(block, axis)  57.3 us
    ppermute x2, waiting for transfers between devices, from_behind(): return lax.ppermute(block, axis, route)  6.51 us
    unnamed x22, local copies, waits for them, and re-layouts  5.2 us
    ppermute x2, starting transfers between devices, from_behind(): return lax.ppermute(block, axis, route)  4.48 us
    dot_general x16, matrix products, along_axis(): jnp.einsum(spec, stacked_table(length), grid_values, preferred_element_ty...  4.37 us
    mul x6, other arithmetic, coulomb(): squares.append(wavenumber * wavenumber)  3.76 us
    another operation x7, other arithmetic  2.56 us
  transfers between devices with their start and end apart: 3, of which 2 were waited for; matrix products, arithmetic and copies ran while one was open for 6% of the time, Pallas kernels for 0%

commit v1 on v0

v1 whole, which is shorter than its diff:
```python
import functools
import math

import jax
import jax.numpy as jnp
import ml_dtypes
import numpy as np
from jax import lax
from jax.experimental import pallas as pl
from jax.experimental.pallas import tpu as pltpu
from jax.sharding import PartitionSpec as P

OCC_DEV = 2
STEPS = 2
KGRID = 4

screening_sq = 0.16
spacing = 0.25
prefactor = -0.5

MESH = pl.DeviceIdType.MESH
CORES = 2


def tables(length):
    indices = np.arange(length)
    angles = (indices[:, None] * indices[None, :] % length) * (2.0 * math.pi / length)

    def rounded(values):
        return values.astype(np.float32).astype(ml_dtypes.bfloat16).astype(np.float32)

    return rounded(np.cos(angles)), rounded(np.sin(angles))


def x_matrices(length, sign_value):
    cosine, sine = tables(length)
    upper = np.concatenate([cosine, -sign_value * sine], axis=1)
    lower = np.concatenate([sign_value * sine, cosine], axis=1)
    plain = np.concatenate([upper, lower], axis=0)
    turned = np.concatenate(
        [sign_value * plain[:, length:], -sign_value * plain[:, :length]], axis=1
    )
    two = np.eye(OCC_DEV, dtype=np.float32)
    return np.stack([np.kron(two, plain), np.kron(two, turned)])


def yz_matrix(grid_y, grid_z):
    cos_y, sin_y = tables(grid_y)
    cos_z, sin_z = tables(grid_z)
    cosine = np.kron(cos_y, cos_z) - np.kron(sin_y, sin_z)
    sine = np.kron(sin_y, cos_z) + np.kron(cos_y, sin_z)
    return np.concatenate([cosine, sine], axis=1)


def slices_of(cells_yz, devices):
    rows = -(-cells_yz // (devices * 16)) * 16
    return rows, -(-cells_yz // rows)


def visit_kernel(k_total, devices, owners_ref, occ_ref, vis_ref, gath, stage, own_out, own_in,
                 send1, recv1, send_own, recv_own, send2, recv2, send3, recv3):
    point = lax.axis_index("ka")
    me = lax.axis_index("band")
    level, core = lax.div(me, CORES), lax.rem(me, CORES)
    levels = devices // CORES
    cells_yz = occ_ref.shape[1]
    rows, count = slices_of(cells_yz, devices)
    overlap = count * rows - cells_yz

    def start_of(device):
        part = lax.rem(device, count)
        return pl.multiple_of(part * rows - lax.div(part, max(count - 1, 1)) * overlap, 16)

    def point_at(distance):
        return lax.rem(point + distance + k_total, k_total)

    def band_at(distance):
        return lax.rem(me + distance + devices, devices)

    def level_at(distance):
        return lax.rem(level + distance + levels, levels)

    barrier = pltpu.get_barrier_semaphore()
    greeted = [(point, band_at(-d)) for d in range(1, devices)]
    for s in range(1, STEPS + 1):
        greeted += [(point_at(-s), level_at(-d) * CORES + core) for d in range(levels)]
        greeted.append((point_at(s), me))
    for device in greeted:
        pl.semaphore_signal(barrier, inc=1, device_id=device, device_id_type=MESH)
    for s in range(STEPS):
        for r in range(OCC_DEV):
            own_out[s, r] = jnp.full((8, 128), owners_ref[0, s, r], jnp.int32).astype(jnp.float32)
    pl.semaphore_wait(barrier, len(greeted))

    owns = []
    for s in range(1, STEPS + 1):
        copy = pltpu.make_async_remote_copy(
            src_ref=own_out.at[s - 1], dst_ref=own_in.at[s - 1],
            send_sem=send_own.at[s - 1], recv_sem=recv_own.at[s - 1],
            device_id=(point_at(-s), me), device_id_type=MESH)
        copy.start()
        owns.append(copy)
    first = []
    for d in range(1, devices):
        target = band_at(d)
        copy = pltpu.make_async_remote_copy(
            src_ref=occ_ref.at[:, pl.ds(start_of(target), rows), :], dst_ref=gath.at[d],
            send_sem=send1.at[d], recv_sem=recv1.at[d],
            device_id=(point, target), device_id_type=MESH)
        copy.start()
        first.append(copy)
    gath[0] = occ_ref[:, pl.ds(start_of(me), rows), :]
    for copy in owns + first:
        copy.wait_recv()

    second, third = [], []

    def place(device):
        return pl.ds(pl.multiple_of(device * rows, 16), rows)

    for s in range(STEPS):
        for r in range(OCC_DEV):
            owner = own_in[s, r]
            chosen = jnp.zeros((rows // 8, 8, 128), jnp.float32)
            for d in range(devices):
                here = (owner == band_at(-d).astype(jnp.float32))[None]
                chosen = jnp.where(
                    here, gath[d, r].astype(jnp.float32).reshape(rows // 8, 8, 128), chosen
                )
            stage[s, r] = chosen.reshape(rows, 128).astype(jnp.bfloat16)
        for d in range(levels):
            copy = pltpu.make_async_remote_copy(
                src_ref=stage.at[s], dst_ref=vis_ref.at[s, :, place(me), :],
                send_sem=send2.at[s, d], recv_sem=recv2.at[s, d],
                device_id=(point_at(s + 1), level_at(d) * CORES + core), device_id_type=MESH)
            copy.start()
            second.append((s, d, copy))
    for s, d, copy in second:
        source = level_at(-d) * CORES + core
        arrived = vis_ref.at[s, :, place(source), :]
        copy.wait_recv()
        across = pltpu.make_async_remote_copy(
            src_ref=arrived, dst_ref=arrived,
            send_sem=send3.at[s, d], recv_sem=recv3.at[s, d],
            device_id=(point, level * CORES + 1 - core), device_id_type=MESH)
        across.start()
        third.append((s, d, across))
    for _, _, copy in third:
        copy.wait_recv()
    for copy in owns + first:
        copy.wait_send()
    for _, _, copy in second + third:
        copy.wait_send()


def visitors(owners, occupied, k_total, devices):
    cells_yz = occupied.shape[1]
    rows, _ = slices_of(cells_yz, devices)
    levels = devices // CORES
    dma = pltpu.SemaphoreType.DMA
    return pl.pallas_call(
        functools.partial(visit_kernel, k_total, devices),
        out_shape=jax.ShapeDtypeStruct((STEPS, OCC_DEV, devices * rows, 128), jnp.bfloat16),
        in_specs=[pl.BlockSpec(memory_space=pltpu.SMEM), pl.BlockSpec(memory_space=pltpu.VMEM)],
        out_specs=pl.BlockSpec(memory_space=pltpu.VMEM),
        scratch_shapes=[
            pltpu.VMEM((devices, OCC_DEV, rows, 128), jnp.bfloat16),
            pltpu.VMEM((STEPS, OCC_DEV, rows, 128), jnp.bfloat16),
            pltpu.VMEM((STEPS, OCC_DEV, 8, 128), jnp.float32),
            pltpu.VMEM((STEPS, OCC_DEV, 8, 128), jnp.float32),
            dma((devices,)), dma((devices,)), dma((STEPS,)), dma((STEPS,)),
            dma((STEPS, levels)), dma((STEPS, levels)),
            dma((STEPS, levels)), dma((STEPS, levels)),
        ],
        compiler_params=pltpu.CompilerParams(
            collective_id=0, has_side_effects=True, vmem_limit_bytes=32 * 1024 * 1024
        ),
    )(owners, occupied)


def exchange_kernel(k_total, devices, grid, waves_ref, umk_ref, t_ref, vis_ref, w_ref, fwd_ref,
                    inv_ref, out_ref, held):
    grid_y, grid_z, grid_x = grid
    cells_yz = grid_y * grid_z
    cells = float(cells_yz * grid_x)
    rows, _ = slices_of(cells_yz, devices)
    whole = cells_yz // rows * rows
    tail = cells_yz - whole
    point = lax.axis_index("ka")
    width = 2 * grid_x
    lane = lax.broadcasted_iota(jnp.int32, (cells_yz, width), 1)
    low = lane < grid_x

    def swap(values):
        return pltpu.roll(values, grid_x, axis=1)

    def square(dim, length, shift):
        shape = (grid_y, grid_z, width)
        index = lax.broadcasted_iota(jnp.int32, shape, dim)
        if dim == 2:
            index = jnp.where(index < grid_x, index, index - grid_x)
        signed = jnp.where(index * 2 < length, index, index - length)
        wave = 2.0 * math.pi / (length * spacing) * (signed.astype(jnp.float32) + shift)
        return wave * wave

    resident = t_ref[...].astype(jnp.float32)
    swapped = swap(resident)
    total = None
    for s in range(STEPS):
        visit = lax.rem(point - (s + 1) + k_total, k_total)
        shift = [
            (waves_ref[point, a] - waves_ref[visit, a]).astype(jnp.float32) / KGRID
            + umk_ref[0, s, a].astype(jnp.float32)
            for a in range(3)
        ]
        squares = (
            square(0, grid_y, shift[1])
            + square(1, grid_z, shift[2])
            + square(2, grid_x, shift[0])
            + screening_sq
        )
        kernel = (4.0 * math.pi / cells / squares).reshape(cells_yz, width)
        re, im, density = [], [], []
        for r in range(OCC_DEV):
            field = vis_ref[s, r, :whole]
            if tail:
                end = whole + rows
                field = jnp.concatenate([field, vis_ref[s, r, end - tail : end]], axis=0)
            field = field.astype(jnp.float32)
            other = swap(field)
            re.append(jnp.where(low, field, other))
            im.append(jnp.where(low, -other, field))
            density.append((re[r] * resident - im[r] * swapped).astype(jnp.bfloat16))
        both = jnp.concatenate(density, axis=1)

        def fourier(fields, x_ref):
            for i in range(2):
                held[i * cells_yz : (i + 1) * cells_yz, :] = jnp.dot(
                    fields, x_ref[i], preferred_element_type=jnp.float32
                ).astype(jnp.bfloat16)
            return jnp.dot(w_ref[...], held[...], preferred_element_type=jnp.float32)

        spectrum = fourier(both, fwd_ref)
        screened = (spectrum * jnp.concatenate([kernel] * OCC_DEV, axis=1)).astype(jnp.bfloat16)
        potential = fourier(screened, inv_ref)
        for r in range(OCC_DEV):
            mine = potential[:, r * width : (r + 1) * width]
            term = re[r] * mine + im[r] * swap(mine)
            total = term if total is None else total + term
    out_ref[...] = (prefactor * total).astype(jnp.bfloat16)


def local(k_total, devices, targets, occupied, wavevectors, umklapp, owners):
    grid_y, grid_z, last_width = targets.shape[2:]
    grid_x = last_width // 2
    cells_yz = grid_y * grid_z
    vis = visitors(owners, occupied.reshape(OCC_DEV, cells_yz, last_width), k_total, devices)
    vmem = pl.BlockSpec(memory_space=pltpu.VMEM)
    smem = pl.BlockSpec(memory_space=pltpu.SMEM)
    out = pl.pallas_call(
        functools.partial(exchange_kernel, k_total, devices, (grid_y, grid_z, grid_x)),
        out_shape=jax.ShapeDtypeStruct((cells_yz, last_width), jnp.bfloat16),
        in_specs=[smem, smem, vmem, vmem, vmem, vmem, vmem],
        out_specs=vmem,
        scratch_shapes=[pltpu.VMEM((2 * cells_yz, OCC_DEV * last_width), jnp.bfloat16)],
        compiler_params=pltpu.CompilerParams(vmem_limit_bytes=32 * 1024 * 1024),
    )(
        wavevectors,
        umklapp,
        targets.reshape(cells_yz, last_width),
        vis,
        jnp.asarray(yz_matrix(grid_y, grid_z).astype(ml_dtypes.bfloat16)),
        jnp.asarray(x_matrices(grid_x, 1.0).astype(ml_dtypes.bfloat16)),
        jnp.asarray(x_matrices(grid_x, -1.0).astype(ml_dtypes.bfloat16)),
    )
    return out.reshape(targets.shape)


def solution(mesh):
    placed = (
        P("ka", "band", None, None, None),
        P("ka", "band", None, None, None),
        P(),
        P("ka", None, None),
        P("ka", None, None),
    )
    return jax.shard_map(
        functools.partial(local, mesh.shape["ka"], mesh.shape["band"]),
        mesh=mesh,
        in_specs=placed,
        out_specs=P("ka", "band", None, None, None),
        check_vma=False,
    )
```

time: 114 us -> 36.3 us (0.32)
  waiting for transfers between devices: 63.8 us -> 0 us
  Pallas kernels: 0 us -> 28.8 us
  between operations: 16.6 us -> 0.02 us
  other arithmetic: 10.8 us -> 0 us
  matrix products: 6.39 us -> 0 us
  starting transfers between devices: 4.49 us -> 0 us
  local copies, waits for them, and re-layouts: 11.3 us -> 7.13 us
    psum x1 -> x0, waiting for transfers between devices: 57.3 us -> none  [spread(): return lax.psum(block, axis)]
    pallas_call x0 -> x2, Pallas kernels: none -> 28.8 us  [the longest x1 24 us: visitors(): pl.pallas_call(functools.partial(visit_kernel, k_total, devices), out_sha...]
    ppermute x2 -> x0, waiting for transfers between devices: 6.51 us -> none  [from_behind(): return lax.ppermute(block, axis, route)]
    dot_general x24 -> x0, matrix products: 6.39 us -> none  [the longest x16 4.37 us: along_axis(): jnp.einsum(spec, stacked_table(length), grid_values, preferred_element_ty...]
    ppermute x2 -> x0, starting transfers between devices: 4.48 us -> none  [from_behind(): return lax.ppermute(block, axis, route)]
    mul x6 -> x0, other arithmetic: 3.76 us -> none  [coulomb(): squares.append(wavenumber * wavenumber)]
    slice x18 -> x0, local copies, waits for them, and re-layouts: 3.57 us -> none  [the longest x16 2.27 us: along_axis(): sin_part[..., half_width:]]
    another operation x7 -> x0, other arithmetic: 2.56 us -> none
  transfers between devices with their start and end apart: 3 -> 0, of which waited for: 2 -> 0; matrix products, arithmetic and copies ran while one was open for 6% -> 0% of each run, Pallas kernels for 0% -> 0%
where the time goes in v1:
time: 36.3 us; the launch traced here: 36 us
  Pallas kernels  28.8 us (79%)
  local copies, waits for them, and re-layouts  7.13 us (20%)
    pallas_call x1, Pallas kernels, visitors(): pl.pallas_call(functools.partial(visit_kernel, k_total, devices), out_sha...  24 us
    unnamed x16, local copies, waits for them, and re-layouts  7.13 us
    pallas_call x1, Pallas kernels, local(): pl.pallas_call(functools.partial(exchange_kernel, k_total, devices, (grid...  4.8 us

profile of v1, /device:TPU:0, one launch (start us, length us, event | category | flops | bytes accessed | tf_op | source)
XLA Modules:
  0.0 36.0 jit_solution(1510117084237794793)
XLA Ops:
  0.0 0.0 copy-start.1
  0.0 1.0 %copy-done.1 = bf16[1,2,24,24,128]{4,3,2,1,0:T(8,128)(2,1)S(1)} copy-done((bf16[1,2,24,24,128]{4,3,2,1,0:T(8,128)(2,1)S(1)}, bf16[1,2,24,24,128]{4,3,2,1,0:T(8,128)(2,1)}, u32[]{:S(2)}) %copy-start.1) | copy-done | bytes 294936
  1.0 0.0 copy-start.6
  1.0 0.7 %copy-done.6 = s32[1,2,2]{2,1,0:T(2,128)S(1)} copy-done((s32[1,2,2]{2,1,0:T(2,128)S(1)}, s32[1,2,2]{2,1,0:T(2,128)}, u32[]{:S(2)}) %copy-start.6) | copy-done | bytes 40
  1.6 24.0 %shard_map.82.vis_ref = bf16[2,2,640,128]{3,2,1,0:T(8,128)(2,1)S(1)} custom-call(s32[1,2,2]{2,1,0:T(2,128)S(1)} %copy-done.6, bf16[2,576,128]{2,1,0:T(8,128)(2,1)S(1)} %bitcast.3), custom_call_target="tpu_custom_call" | custom-call | tf_op jit(solution)/shard_map/pallas_call | solution.py:161
  25.7 0.0 copy-start
  25.7 1.3 %copy-done = bf16[576,1152]{1,0:T(8,128)(2,1)S(1)} copy-done((bf16[576,1152]{1,0:T(8,128)(2,1)S(1)}, bf16[576,1152]{1,0:T(8,128)(2,1)}, u32[]{:S(2)}) %copy-start) | copy-done | bytes 1327128
  27.0 0.0 copy-start.2
  27.0 0.9 %copy-done.2 = bf16[2,256,256]{2,1,0:T(8,128)(2,1)S(1)} copy-done((bf16[2,256,256]{2,1,0:T(8,128)(2,1)S(1)}, bf16[2,256,256]{2,1,0:T(8,128)(2,1)}, u32[]{:S(2)}) %copy-start.2) | copy-done | bytes 262168
  27.9 0.0 copy-start.3
  27.9 0.9 %copy-done.3 = bf16[2,256,256]{2,1,0:T(8,128)(2,1)S(1)} copy-done((bf16[2,256,256]{2,1,0:T(8,128)(2,1)S(1)}, bf16[2,256,256]{2,1,0:T(8,128)(2,1)}, u32[]{:S(2)}) %copy-start.3) | copy-done | bytes 262168
  28.9 0.0 copy-start.4
  28.9 0.9 %copy-done.4 = bf16[1,1,24,24,128]{4,3,2,1,0:T(8,128)(2,1)S(1)} copy-done((bf16[1,1,24,24,128]{4,3,2,1,0:T(8,128)(2,1)S(1)}, bf16[1,1,24,24,128]{4,3,2,1,0:T(8,128)(2,1)}, u32[]{:S(2)}) %copy-start.4) | copy-done | bytes 147480
  29.8 0.0 copy-start.5
  29.8 0.7 %copy-done.5 = s32[4,3]{1,0:T(4,128)S(1)} copy-done((s32[4,3]{1,0:T(4,128)S(1)}, s32[4,3]{1,0:T(4,128)}, u32[]{:S(2)}) %copy-start.5) | copy-done | bytes 72
  30.5 0.0 copy-start.7
  30.5 0.7 %copy-done.7 = s32[1,2,3]{2,1,0:T(2,128)S(1)} copy-done((s32[1,2,3]{2,1,0:T(2,128)S(1)}, s32[1,2,3]{2,1,0:T(2,128)}, u32[]{:S(2)}) %copy-start.7) | copy-done | bytes 48
  31.2 4.8 %shard_map.83 = bf16[576,128]{1,0:T(8,128)(2,1)} custom-call(s32[4,3]{1,0:T(4,128)S(1)} %copy-done.5, s32[1,2,3]{2,1,0:T(2,128)S(1)} %copy-done.7, bf16[576,128]{1,0:T(8,128)(2,1)S(1)} %bitcast.4, bf16[2,2,640,128]{3,2,1,0:T(8,128)(2,1)S(1)} %shard_map.82.vis_ref, bf16[576,1152]{1,0:T(8,128)(2,1)S(1)} %copy-done, bf16[2,256,256]{2,1,0:T(8,128)(2,1)S(1)} %copy-done.3, ...), custom_call_target="tpu_custom_call" | custom-call | tf_op jit(solution)/shard_map/pallas_call | solution.py:260
Async XLA Ops:
  0.0 1.0 %copy-start.1 = (bf16[1,2,24,24,128]{4,3,2,1,0:T(8,128)(2,1)S(1)}, bf16[1,2,24,24,128]{4,3,2,1,0:T(8,128)(2,1)}, u32[]{:S(2)}) copy-start(bf16[1,2,24,24,128]{4,3,2,1,0:T(8,128)(2,1)} %param.9) | copy-start | bytes 884740
  1.0 0.7 %copy-start.6 = (s32[1,2,2]{2,1,0:T(2,128)S(1)}, s32[1,2,2]{2,1,0:T(2,128)}, u32[]{:S(2)}) copy-start(s32[1,2,2]{2,1,0:T(2,128)} %owners_ref.1) | copy-start | bytes 52
  25.7 1.3 %copy-start = (bf16[576,1152]{1,0:T(8,128)(2,1)S(1)}, bf16[576,1152]{1,0:T(8,128)(2,1)}, u32[]{:S(2)}) copy-start(bf16[576,1152]{1,0:T(8,128)(2,1)} %constant.6.clone.w_ref) | copy-start | bytes 3981316
  27.0 0.9 %copy-start.2 = (bf16[2,256,256]{2,1,0:T(8,128)(2,1)S(1)}, bf16[2,256,256]{2,1,0:T(8,128)(2,1)}, u32[]{:S(2)}) copy-start(bf16[2,256,256]{2,1,0:T(8,128)(2,1)} %constant.8.clone.inv_ref) | copy-start | bytes 786436
  27.9 0.9 %copy-start.3 = (bf16[2,256,256]{2,1,0:T(8,128)(2,1)S(1)}, bf16[2,256,256]{2,1,0:T(8,128)(2,1)}, u32[]{:S(2)}) copy-start(bf16[2,256,256]{2,1,0:T(8,128)(2,1)} %constant.7.clone.fwd_ref) | copy-start | bytes 786436
  28.9 0.9 %copy-start.4 = (bf16[1,1,24,24,128]{4,3,2,1,0:T(8,128)(2,1)S(1)}, bf16[1,1,24,24,128]{4,3,2,1,0:T(8,128)(2,1)}, u32[]{:S(2)}) copy-start(bf16[1,1,24,24,128]{4,3,2,1,0:T(8,128)(2,1)} %param.8) | copy-start | bytes 442372
  29.8 0.7 %copy-start.5 = (s32[4,3]{1,0:T(4,128)S(1)}, s32[4,3]{1,0:T(4,128)}, u32[]{:S(2)}) copy-start(s32[4,3]{1,0:T(4,128)} %waves_ref.1) | copy-start | bytes 148
  30.5 0.7 %copy-start.7 = (s32[1,2,3]{2,1,0:T(2,128)S(1)}, s32[1,2,3]{2,1,0:T(2,128)}, u32[]{:S(2)}) copy-start(s32[1,2,3]{2,1,0:T(2,128)} %umk_ref.1) | copy-start | bytes 76

commit v2 on v1

v2 whole, which is shorter than its diff:
```python
import functools
import math

import jax
import jax.numpy as jnp
import ml_dtypes
import numpy as np
from jax import lax
from jax.experimental import pallas as pl
from jax.experimental.pallas import tpu as pltpu
from jax.sharding import PartitionSpec as P

OCC_DEV = 2
STEPS = 2
KGRID = 4

screening_sq = 0.16
spacing = 0.25
prefactor = -0.5

MESH = pl.DeviceIdType.MESH
CORES = 2


def tables(length):
    indices = np.arange(length)
    angles = (indices[:, None] * indices[None, :] % length) * (2.0 * math.pi / length)

    def rounded(values):
        return values.astype(np.float32).astype(ml_dtypes.bfloat16).astype(np.float32)

    return rounded(np.cos(angles)), rounded(np.sin(angles))


def x_matrices(length, sign_value):
    cosine, sine = tables(length)
    upper = np.concatenate([cosine, -sign_value * sine], axis=1)
    lower = np.concatenate([sign_value * sine, cosine], axis=1)
    plain = np.concatenate([upper, lower], axis=0)
    turned = np.concatenate(
        [sign_value * plain[:, length:], -sign_value * plain[:, :length]], axis=1
    )
    two = np.eye(OCC_DEV, dtype=np.float32)
    return np.stack([np.kron(two, plain), np.kron(two, turned)])


def yz_matrix(grid_y, grid_z):
    cos_y, sin_y = tables(grid_y)
    cos_z, sin_z = tables(grid_z)
    cosine = np.kron(cos_y, cos_z) - np.kron(sin_y, sin_z)
    sine = np.kron(sin_y, cos_z) + np.kron(cos_y, sin_z)
    return np.concatenate([cosine, sine], axis=1)


def slices_of(cells_yz, devices):
    rows = -(-cells_yz // (devices * 16)) * 16
    return rows, -(-cells_yz // rows)


def exchange_kernel(k_total, devices, grid, owners_hbm, waves_hbm, umk_hbm, occ_hbm, t_hbm, w_hbm,
                    fwd_hbm, inv_hbm, out_ref, owners_ref, waves_ref, umk_ref, occ_ref, t_ref,
                    w_ref, fwd_ref, inv_ref, vis_ref, gath, stage, own_out, own_in, held, coul,
                    load, send1, recv1, send_own, recv_own, send2, recv2, send3, recv3):
    point = lax.axis_index("ka")
    me = lax.axis_index("band")
    level, core = lax.div(me, CORES), lax.rem(me, CORES)
    levels = devices // CORES
    grid_y, grid_z, grid_x = grid
    width = 2 * grid_x
    cells_yz = grid_y * grid_z
    cells = float(cells_yz * grid_x)
    rows, count = slices_of(cells_yz, devices)
    overlap = count * rows - cells_yz
    whole = cells_yz // rows * rows
    tail = cells_yz - whole

    loads = [
        pltpu.make_async_copy(source, target, load.at[i])
        for i, (source, target) in enumerate((
            (owners_hbm, owners_ref), (occ_hbm, occ_ref), (waves_hbm, waves_ref),
            (umk_hbm, umk_ref), (t_hbm, t_ref), (fwd_hbm, fwd_ref), (w_hbm, w_ref),
            (inv_hbm, inv_ref),
        ))
    ]
    for copy in loads:
        copy.start()

    def start_of(device):
        part = lax.rem(device, count)
        return pl.multiple_of(part * rows - lax.div(part, max(count - 1, 1)) * overlap, 16)

    def point_at(distance):
        return lax.rem(point + distance + k_total, k_total)

    def band_at(distance):
        return lax.rem(me + distance + devices, devices)

    def level_at(distance):
        return lax.rem(level + distance + levels, levels)

    barrier = pltpu.get_barrier_semaphore()
    greeted = [(point, band_at(-d)) for d in range(1, devices)]
    for s in range(1, STEPS + 1):
        greeted += [(point_at(-s), level_at(-d) * CORES + core) for d in range(levels)]
        greeted.append((point_at(s), me))
    for device in greeted:
        pl.semaphore_signal(barrier, inc=1, device_id=device, device_id_type=MESH)
    loads[0].wait()
    for s in range(STEPS):
        for r in range(OCC_DEV):
            own_out[s, r] = jnp.full((8, 128), owners_ref[0, s, r], jnp.int32).astype(jnp.float32)
    loads[1].wait()
    pl.semaphore_wait(barrier, len(greeted))

    owns = []
    for s in range(1, STEPS + 1):
        copy = pltpu.make_async_remote_copy(
            src_ref=own_out.at[s - 1], dst_ref=own_in.at[s - 1],
            send_sem=send_own.at[s - 1], recv_sem=recv_own.at[s - 1],
            device_id=(point_at(-s), me), device_id_type=MESH)
        copy.start()
        owns.append(copy)
    first = []
    for d in range(1, devices):
        target = band_at(d)
        copy = pltpu.make_async_remote_copy(
            src_ref=occ_ref.at[:, pl.ds(start_of(target), rows), :], dst_ref=gath.at[d],
            send_sem=send1.at[d], recv_sem=recv1.at[d],
            device_id=(point, target), device_id_type=MESH)
        copy.start()
        first.append(copy)
    gath[0] = occ_ref[:, pl.ds(start_of(me), rows), :]

    def swap(values):
        return pltpu.roll(values, grid_x, axis=1)

    def square(dim, length, shift):
        shape = (grid_y, grid_z, width)
        index = lax.broadcasted_iota(jnp.int32, shape, dim)
        if dim == 2:
            index = jnp.where(index < grid_x, index, index - grid_x)
        signed = jnp.where(index * 2 < length, index, index - length)
        wave = 2.0 * math.pi / (length * spacing) * (signed.astype(jnp.float32) + shift)
        return wave * wave

    for copy in loads[2:]:
        copy.wait()
    for s in range(STEPS):
        visit = point_at(-(s + 1))
        shift = [
            (waves_ref[point, a] - waves_ref[visit, a]).astype(jnp.float32) / KGRID
            + umk_ref[0, s, a].astype(jnp.float32)
            for a in range(3)
        ]
        squares = (
            square(0, grid_y, shift[1])
            + square(1, grid_z, shift[2])
            + square(2, grid_x, shift[0])
            + screening_sq
        )
        coul[s] = (4.0 * math.pi / cells / squares).reshape(cells_yz, width)

    for copy in owns + first:
        copy.wait_recv()

    def place(device):
        return pl.ds(pl.multiple_of(device * rows, 16), rows)

    second = [[] for _ in range(STEPS)]
    third = [[] for _ in range(STEPS)]
    for s in range(STEPS):
        for r in range(OCC_DEV):
            owner = own_in[s, r]
            chosen = jnp.zeros((rows // 8, 8, 128), jnp.float32)
            for d in range(devices):
                here = (owner == band_at(-d).astype(jnp.float32))[None]
                chosen = jnp.where(
                    here, gath[d, r].astype(jnp.float32).reshape(rows // 8, 8, 128), chosen
                )
            stage[s, r] = chosen.reshape(rows, 128).astype(jnp.bfloat16)
        for d in range(levels):
            copy = pltpu.make_async_remote_copy(
                src_ref=stage.at[s], dst_ref=vis_ref.at[s, :, place(me), :],
                send_sem=send2.at[s, d], recv_sem=recv2.at[s, d],
                device_id=(point_at(s + 1), level_at(d) * CORES + core), device_id_type=MESH)
            copy.start()
            second[s].append(copy)

    def pass_on(s):
        for d, copy in enumerate(second[s]):
            copy.wait_recv()
            arrived = vis_ref.at[s, :, place(level_at(-d) * CORES + core), :]
            across = pltpu.make_async_remote_copy(
                src_ref=arrived, dst_ref=arrived,
                send_sem=send3.at[s, d], recv_sem=recv3.at[s, d],
                device_id=(point, level * CORES + 1 - core), device_id_type=MESH)
            across.start()
            third[s].append(across)

    low = lax.broadcasted_iota(jnp.int32, (cells_yz, width), 1) < grid_x

    def fourier(fields, x_ref):
        for i in range(2):
            held[i * cells_yz : (i + 1) * cells_yz, :] = jnp.dot(
                fields, x_ref[i], preferred_element_type=jnp.float32
            ).astype(jnp.bfloat16)
        return jnp.dot(w_ref[...], held[...], preferred_element_type=jnp.float32)

    total = None
    for s in range(STEPS):
        pass_on(s)
        for copy in third[s]:
            copy.wait_recv()
        resident = t_ref[...].astype(jnp.float32)
        swapped = swap(resident)
        re, im, density = [], [], []
        for r in range(OCC_DEV):
            field = vis_ref[s, r, :whole]
            if tail:
                end = whole + rows
                field = jnp.concatenate([field, vis_ref[s, r, end - tail : end]], axis=0)
            field = field.astype(jnp.float32)
            other = swap(field)
            re.append(jnp.where(low, field, other))
            im.append(jnp.where(low, -other, field))
            density.append((re[r] * resident - im[r] * swapped).astype(jnp.bfloat16))
        spectrum = fourier(jnp.concatenate(density, axis=1), fwd_ref)
        kernel = coul[s]
        screened = (spectrum * jnp.concatenate([kernel] * OCC_DEV, axis=1)).astype(jnp.bfloat16)
        potential = fourier(screened, inv_ref)
        for r in range(OCC_DEV):
            mine = potential[:, r * width : (r + 1) * width]
            term = re[r] * mine + im[r] * swap(mine)
            total = term if total is None else total + term
    out_ref[...] = (prefactor * total).astype(jnp.bfloat16)
    for copy in owns + first + second[0] + second[1] + third[0] + third[1]:
        copy.wait_send()


def local(k_total, devices, targets, occupied, wavevectors, umklapp, owners):
    grid_y, grid_z, last_width = targets.shape[2:]
    grid_x = last_width // 2
    cells_yz = grid_y * grid_z
    rows, _ = slices_of(cells_yz, devices)
    levels = devices // CORES
    dma = pltpu.SemaphoreType.DMA
    hbm = pl.BlockSpec(memory_space=pltpu.HBM)
    args = (
        owners,
        wavevectors,
        umklapp,
        occupied.reshape(OCC_DEV, cells_yz, last_width),
        targets.reshape(cells_yz, last_width),
        jnp.asarray(yz_matrix(grid_y, grid_z).astype(ml_dtypes.bfloat16)),
        jnp.asarray(x_matrices(grid_x, 1.0).astype(ml_dtypes.bfloat16)),
        jnp.asarray(x_matrices(grid_x, -1.0).astype(ml_dtypes.bfloat16)),
    )
    out = pl.pallas_call(
        functools.partial(exchange_kernel, k_total, devices, (grid_y, grid_z, grid_x)),
        out_shape=jax.ShapeDtypeStruct((cells_yz, last_width), jnp.bfloat16),
        in_specs=[hbm] * len(args),
        out_specs=pl.BlockSpec(memory_space=pltpu.VMEM),
        scratch_shapes=[pltpu.SMEM(x.shape, x.dtype) for x in args[:3]]
        + [pltpu.VMEM(x.shape, x.dtype) for x in args[3:]]
        + [
            pltpu.VMEM((STEPS, OCC_DEV, devices * rows, 128), jnp.bfloat16),
            pltpu.VMEM((devices, OCC_DEV, rows, 128), jnp.bfloat16),
            pltpu.VMEM((STEPS, OCC_DEV, rows, 128), jnp.bfloat16),
            pltpu.VMEM((STEPS, OCC_DEV, 8, 128), jnp.float32),
            pltpu.VMEM((STEPS, OCC_DEV, 8, 128), jnp.float32),
            pltpu.VMEM((2 * cells_yz, OCC_DEV * last_width), jnp.bfloat16),
            pltpu.VMEM((STEPS, cells_yz, last_width), jnp.float32),
            dma((len(args),)),
            dma((devices,)), dma((devices,)), dma((STEPS,)), dma((STEPS,)),
            dma((STEPS, levels)), dma((STEPS, levels)),
            dma((STEPS, levels)), dma((STEPS, levels)),
        ],
        compiler_params=pltpu.CompilerParams(
            collective_id=0, has_side_effects=True, vmem_limit_bytes=62 * 1024 * 1024
        ),
    )(*args)
    return out.reshape(targets.shape)


def solution(mesh):
    placed = (
        P("ka", "band", None, None, None),
        P("ka", "band", None, None, None),
        P(),
        P("ka", None, None),
        P("ka", None, None),
    )
    return jax.shard_map(
        functools.partial(local, mesh.shape["ka"], mesh.shape["band"]),
        mesh=mesh,
        in_specs=placed,
        out_specs=P("ka", "band", None, None, None),
        check_vma=False,
    )
```

time: 36.3 us -> 30.5 us (0.84)
  local copies, waits for them, and re-layouts: 7.13 us -> 1.59 us
    pallas_call x1 -> x0, Pallas kernels: 24 us -> none  [visitors(): pl.pallas_call(functools.partial(visit_kernel, k_total, devices), out_sha...]
    pallas_call x1, Pallas kernels: 4.8 us -> 28.7 us  [local(): pl.pallas_call(functools.partial(exchange_kernel, k_total, devices, (grid...]
    unnamed x16 -> x1, local copies, waits for them, and re-layouts: 7.13 us -> 1.59 us
where the time goes in v2:
time: 30.5 us; the launch traced here: 30.3 us
  Pallas kernels  28.7 us (94%)
  local copies, waits for them, and re-layouts  1.59 us (5%)
    pallas_call x1, Pallas kernels, local(): pl.pallas_call(functools.partial(exchange_kernel, k_total, devices, (grid...  28.7 us
    unnamed x1, local copies, waits for them, and re-layouts  1.59 us

profile of v2, /device:TPU:0, one launch (start us, length us, event | category | flops | bytes accessed | tf_op | source)
XLA Modules:
  0.0 30.3 jit_solution(7836430369467186643)
XLA Ops:
  0.0 28.7 %shard_map.82 = bf16[576,128]{1,0:T(8,128)(2,1)} custom-call(s32[1,2,2]{2,1,0:T(2,128)} %owners_hbm.1, s32[4,3]{1,0:T(4,128)} %waves_hbm.1, s32[1,2,3]{2,1,0:T(2,128)} %umk_hbm.1, bf16[2,576,128]{2,1,0:T(8,128)(2,1)} %bitcast.4, bf16[576,128]{1,0:T(8,128)(2,1)} %bitcast.5, bf16[576,1152]{1,0:T(8,128)(2,1)} %constant.6.clone.w_hbm, ...), custom_call_target="tpu_custom_call" | custom-call | tf_op jit(solution)/shard_map/pallas_call | solution.py:258
  28.8 1.6 %copy.10 = bf16[1,1,24,24,128]{4,3,2,1,0:T(8,128)(2,1)} copy(bf16[1,1,24,24,128]{4,3,2,1,0:T(8,128)(2,1)} %bitcast.3) | data formatting | bytes 294912

commit v3 on v2

--- a/solution.py
+++ b/solution.py
@@ -40,7 +40,7 @@
     turned = np.concatenate(
         [sign_value * plain[:, length:], -sign_value * plain[:, :length]], axis=1
     )
-    two = np.eye(OCC_DEV, dtype=np.float32)
+    two = np.eye(STEPS, dtype=np.float32)
     return np.stack([np.kron(two, plain), np.kron(two, turned)])
 
 
@@ -120,15 +120,16 @@
             device_id=(point_at(-s), me), device_id_type=MESH)
         copy.start()
         owns.append(copy)
-    first = []
-    for d in range(1, devices):
-        target = band_at(d)
-        copy = pltpu.make_async_remote_copy(
-            src_ref=occ_ref.at[:, pl.ds(start_of(target), rows), :], dst_ref=gath.at[d],
-            send_sem=send1.at[d], recv_sem=recv1.at[d],
-            device_id=(point, target), device_id_type=MESH)
-        copy.start()
-        first.append(copy)
+    first = [[] for _ in range(OCC_DEV)]
+    for r in range(OCC_DEV):
+        for d in range(1, devices):
+            target = band_at(d)
+            copy = pltpu.make_async_remote_copy(
+                src_ref=occ_ref.at[r, pl.ds(start_of(target), rows), :], dst_ref=gath.at[d, r],
+                send_sem=send1.at[r, d], recv_sem=recv1.at[r, d],
+                device_id=(point, target), device_id_type=MESH)
+            copy.start()
+            first[r].append(copy)
     gath[0] = occ_ref[:, pl.ds(start_of(me), rows), :]
 
     def swap(values):
@@ -160,16 +161,15 @@
         )
         coul[s] = (4.0 * math.pi / cells / squares).reshape(cells_yz, width)
 
-    for copy in owns + first:
-        copy.wait_recv()
-
     def place(device):
         return pl.ds(pl.multiple_of(device * rows, 16), rows)
 
-    second = [[] for _ in range(STEPS)]
-    third = [[] for _ in range(STEPS)]
-    for s in range(STEPS):
-        for r in range(OCC_DEV):
+    second = [[] for _ in range(OCC_DEV)]
+    third = [[] for _ in range(OCC_DEV)]
+    for r in range(OCC_DEV):
+        for copy in (owns if r == 0 else []) + first[r]:
+            copy.wait_recv()
+        for s in range(STEPS):
             owner = own_in[s, r]
             chosen = jnp.zeros((rows // 8, 8, 128), jnp.float32)
             for d in range(devices):
@@ -178,24 +178,24 @@
                     here, gath[d, r].astype(jnp.float32).reshape(rows // 8, 8, 128), chosen
                 )
             stage[s, r] = chosen.reshape(rows, 128).astype(jnp.bfloat16)
-        for d in range(levels):
-            copy = pltpu.make_async_remote_copy(
-                src_ref=stage.at[s], dst_ref=vis_ref.at[s, :, place(me), :],
-                send_sem=send2.at[s, d], recv_sem=recv2.at[s, d],
-                device_id=(point_at(s + 1), level_at(d) * CORES + core), device_id_type=MESH)
-            copy.start()
-            second[s].append(copy)
-
-    def pass_on(s):
-        for d, copy in enumerate(second[s]):
+            for d in range(levels):
+                copy = pltpu.make_async_remote_copy(
+                    src_ref=stage.at[s, r], dst_ref=vis_ref.at[s, r, place(me), :],
+                    send_sem=send2.at[r, s, d], recv_sem=recv2.at[r, s, d],
+                    device_id=(point_at(s + 1), level_at(d) * CORES + core), device_id_type=MESH)
+                copy.start()
+                second[r].append((s, d, copy))
+
+    def pass_on(r):
+        for s, d, copy in second[r]:
             copy.wait_recv()
-            arrived = vis_ref.at[s, :, place(level_at(-d) * CORES + core), :]
+            arrived = vis_ref.at[s, r, place(level_at(-d) * CORES + core), :]
             across = pltpu.make_async_remote_copy(
                 src_ref=arrived, dst_ref=arrived,
-                send_sem=send3.at[s, d], recv_sem=recv3.at[s, d],
+                send_sem=send3.at[r, s, d], recv_sem=recv3.at[r, s, d],
                 device_id=(point, level * CORES + 1 - core), device_id_type=MESH)
             across.start()
-            third[s].append(across)
+            third[r].append(across)
 
     low = lax.broadcasted_iota(jnp.int32, (cells_yz, width), 1) < grid_x
 
@@ -207,14 +207,15 @@
         return jnp.dot(w_ref[...], held[...], preferred_element_type=jnp.float32)
 
     total = None
-    for s in range(STEPS):
-        pass_on(s)
-        for copy in third[s]:
+    kernel = jnp.concatenate([coul[s] for s in range(STEPS)], axis=1)
+    for r in range(OCC_DEV):
+        pass_on(r)
+        for copy in third[r]:
             copy.wait_recv()
         resident = t_ref[...].astype(jnp.float32)
         swapped = swap(resident)
         re, im, density = [], [], []
-        for r in range(OCC_DEV):
+        for s in range(STEPS):
             field = vis_ref[s, r, :whole]
             if tail:
                 end = whole + rows
@@ -223,18 +224,19 @@
             other = swap(field)
             re.append(jnp.where(low, field, other))
             im.append(jnp.where(low, -other, field))
-            density.append((re[r] * resident - im[r] * swapped).astype(jnp.bfloat16))
+            density.append((re[s] * resident - im[s] * swapped).astype(jnp.bfloat16))
         spectrum = fourier(jnp.concatenate(density, axis=1), fwd_ref)
-        kernel = coul[s]
-        screened = (spectrum * jnp.concatenate([kernel] * OCC_DEV, axis=1)).astype(jnp.bfloat16)
-        potential = fourier(screened, inv_ref)
-        for r in range(OCC_DEV):
-            mine = potential[:, r * width : (r + 1) * width]
-            term = re[r] * mine + im[r] * swap(mine)
+        potential = fourier((spectrum * kernel).astype(jnp.bfloat16), inv_ref)
+        for s in range(STEPS):
+            mine = potential[:, s * width : (s + 1) * width]
+            term = re[s] * mine + im[s] * swap(mine)
             total = term if total is None else total + term
     out_ref[...] = (prefactor * total).astype(jnp.bfloat16)
-    for copy in owns + first + second[0] + second[1] + third[0] + third[1]:
+    for copy in owns:
         copy.wait_send()
+    for r in range(OCC_DEV):
+        for copy in first[r] + [entry[-1] for entry in second[r]] + third[r]:
+            copy.wait_send()
 
 
 def local(k_total, devices, targets, occupied, wavevectors, umklapp, owners):
@@ -268,12 +270,12 @@
             pltpu.VMEM((STEPS, OCC_DEV, rows, 128), jnp.bfloat16),
             pltpu.VMEM((STEPS, OCC_DEV, 8, 128), jnp.float32),
             pltpu.VMEM((STEPS, OCC_DEV, 8, 128), jnp.float32),
-            pltpu.VMEM((2 * cells_yz, OCC_DEV * last_width), jnp.bfloat16),
+            pltpu.VMEM((2 * cells_yz, STEPS * last_width), jnp.bfloat16),
             pltpu.VMEM((STEPS, cells_yz, last_width), jnp.float32),
             dma((len(args),)),
-            dma((devices,)), dma((devices,)), dma((STEPS,)), dma((STEPS,)),
-            dma((STEPS, levels)), dma((STEPS, levels)),
-            dma((STEPS, levels)), dma((STEPS, levels)),
+            dma((OCC_DEV, devices)), dma((OCC_DEV, devices)), dma((STEPS,)), dma((STEPS,)),
+            dma((OCC_DEV, STEPS, levels)), dma((OCC_DEV, STEPS, levels)),
+            dma((OCC_DEV, STEPS, levels)), dma((OCC_DEV, STEPS, levels)),
         ],
         compiler_params=pltpu.CompilerParams(
             collective_id=0, has_side_effects=True, vmem_limit_bytes=62 * 1024 * 1024

time: 30.5 us -> 29.4 us (0.964)
  Pallas kernels: 28.7 us -> 27.7 us
    pallas_call x1, Pallas kernels: 28.7 us -> 27.7 us  [local(): pl.pallas_call(functools.partial(exchange_kernel, k_total, devices, (grid...]
where the time goes in v3:
time: 29.4 us; the launch traced here: 29.3 us
  Pallas kernels  27.7 us (94%)
  local copies, waits for them, and re-layouts  1.59 us (5%)
    pallas_call x1, Pallas kernels, local(): pl.pallas_call(functools.partial(exchange_kernel, k_total, devices, (grid...  27.7 us
    unnamed x1, local copies, waits for them, and re-layouts  1.59 us

profile of v3, /device:TPU:0, one launch (start us, length us, event | category | flops | bytes accessed | tf_op | source)
XLA Modules:
  0.0 29.3 jit_solution(11177107618216276159)
XLA Ops:
  0.0 27.7 %shard_map.82 = bf16[576,128]{1,0:T(8,128)(2,1)} custom-call(s32[1,2,2]{2,1,0:T(2,128)} %owners_hbm.1, s32[4,3]{1,0:T(4,128)} %waves_hbm.1, s32[1,2,3]{2,1,0:T(2,128)} %umk_hbm.1, bf16[2,576,128]{2,1,0:T(8,128)(2,1)} %bitcast.4, bf16[576,128]{1,0:T(8,128)(2,1)} %bitcast.5, bf16[576,1152]{1,0:T(8,128)(2,1)} %constant.6.clone.w_hbm, ...), custom_call_target="tpu_custom_call" | custom-call | tf_op jit(solution)/shard_map/pallas_call | solution.py:260
  27.7 1.6 %copy.10 = bf16[1,1,24,24,128]{4,3,2,1,0:T(8,128)(2,1)} copy(bf16[1,1,24,24,128]{4,3,2,1,0:T(8,128)(2,1)} %bitcast.3) | data formatting | bytes 294912
